TPU v7x, 256 devices: a whole 4x4x8 slice. The times are simulated.
256 devices in a mesh: rep: 16 (over x, y), seq: 16 (over z, core).
Axes of the slice: x: 4, y: 4, z: 8, core: 2. Of those that a mesh axis runs over, the one named last changes fastest.
Arguments:
- queries: bfloat16 [16, 2048, 4096], P('rep', 'seq'), may hold values from -6 to 6
- key_rows: bfloat16 [16, 2048, 4096], P('rep', 'seq'), may hold values from -6 to 6
- value_rows: bfloat16 [16, 2048, 4096], P('rep', 'seq'), may hold values from -6 to 6
- cotangent: bfloat16 [16, 2048, 3584], P('rep', 'seq'), may hold values from -0.09375 to 0.09375
- numerators: bfloat16 [16, 4096, 3584], P('rep', 'seq'), may hold values from -6 to 6
- push_weights: float32 [16], P('rep'), may hold values from 0.5 to 2
- doc_ids: int32 [16, 2048], P('rep'), may hold values from 0 to 3, never falling along the last dimension, each value on 1 to 1024 neighbouring positions
- out_links: int32 [16, 16], replicated, may hold values from 0 to 1, as said below
- denominators: int32 [16], replicated, may hold values from 2 to 6, as said below
Outputs:
- query_grads: bfloat16 [16, 2048, 4096], P('rep', 'seq')
- key_grads: bfloat16 [16, 2048, 4096], P('rep', 'seq')
- value_grads: bfloat16 [16, 2048, 4096], P('rep', 'seq')
- mixed_numerators: bfloat16 [16, 4096, 3584], P('rep', 'seq')
- mixed_weights: float32 [16], P('rep')
Inputs may be any that keep to these rules, and one draw needn't show every extreme that they name: out_links[r, c] is 1 only where c = (r + 2^b) mod 16 for some b with 2^b < 16; every replica has one or more out-neighbours. denominators[r] is one or two more than the number of out-neighbours of replica r.
All inputs are finite; a program needn't handle non-finite values.
Results may differ from a plain program's by a relative error of at most 0.035.
Values may be sent and summed in bfloat16 or wider, within the bound.
A program may use at most 128 MiB of HBM per device.

v0:
```python
import math

import jax
import jax.numpy as jnp
from jax import lax
from jax.sharding import PartitionSpec as P

HEAD_DIM = 128


step_size = 3.0


def shifted(shard, axis, by):
    peers = lax.axis_size(axis)
    return lax.ppermute(shard, axis, [(i, (i + by) % peers) for i in range(peers)])


def block_layout(seq_len):
    blocks = max(1, min(8, seq_len // 512))
    return (blocks, seq_len // blocks)


def pick_entry(table, index):
    return jnp.sum(jnp.where(jnp.arange(table.shape[0]) == index, table, jnp.zeros_like(table)))


def attend_forward(query_heads, key_heads, value_heads, doc_row):
    seq_len = query_heads.shape[0]
    blocks, block_len = block_layout(seq_len)
    scale_factor = 1.0 / math.sqrt(HEAD_DIM)
    positions = jnp.arange(seq_len)
    prob_blocks = []
    out_blocks = []
    for block_id in range(blocks):
        row_start = block_id * block_len
        row_end = row_start + block_len
        scores = (
            jnp.einsum(
                "qhd,khd->hqk",
                query_heads[row_start:row_end],
                key_heads[:row_end],
                preferred_element_type=jnp.float32,
            )
            * scale_factor
        )
        allowed = (positions[None, :row_end] <= positions[row_start:row_end, None]) & (
            doc_row[None, :row_end] == doc_row[row_start:row_end, None]
        )
        scores = jnp.where(allowed[None], scores, -jnp.inf)
        row_peak = jnp.max(scores, axis=2, keepdims=True)
        exponent = jnp.exp(scores - row_peak)
        probs_bf = (exponent / jnp.sum(exponent, axis=2, keepdims=True)).astype(jnp.bfloat16)
        prob_blocks.append(probs_bf)
        out_blocks.append(
            jnp.einsum(
                "hqk,khd->qhd", probs_bf, value_heads[:row_end], preferred_element_type=jnp.float32
            ).astype(jnp.bfloat16)
        )
    return (prob_blocks, jnp.concatenate(out_blocks, axis=0))


def attend_backward(query_heads, key_heads, value_heads, prob_blocks, attended, grad_heads):
    seq_len = query_heads.shape[0]
    blocks, block_len = block_layout(seq_len)
    scale_factor = 1.0 / math.sqrt(HEAD_DIM)
    key_acc = jnp.zeros(key_heads.shape, jnp.float32)
    value_acc = jnp.zeros(value_heads.shape, jnp.float32)
    query_parts = []
    for block_id in range(blocks):
        row_start = block_id * block_len
        row_end = row_start + block_len
        probs_bf = prob_blocks[block_id]
        grad_block = grad_heads[row_start:row_end]
        value_acc = value_acc.at[:row_end].add(
            jnp.einsum("hqk,qhd->khd", probs_bf, grad_block, preferred_element_type=jnp.float32)
        )
        grad_probs = jnp.einsum(
            "qhd,khd->hqk", grad_block, value_heads[:row_end], preferred_element_type=jnp.float32
        )
        centre = jnp.einsum(
            "qhd,qhd->hq",
            grad_block,
            attended[row_start:row_end],
            preferred_element_type=jnp.float32,
        )
        grad_scores = (probs_bf.astype(jnp.float32) * (grad_probs - centre[:, :, None])).astype(
            jnp.bfloat16
        )
        query_parts.append(
            (
                jnp.einsum(
                    "hqk,khd->qhd",
                    grad_scores,
                    key_heads[:row_end],
                    preferred_element_type=jnp.float32,
                )
                * scale_factor
            ).astype(jnp.bfloat16)
        )
        key_acc = key_acc.at[:row_end].add(
            jnp.einsum(
                "hqk,qhd->khd",
                grad_scores,
                query_heads[row_start:row_end],
                preferred_element_type=jnp.float32,
            )
            * scale_factor
        )
    return (
        jnp.concatenate(query_parts, axis=0),
        key_acc.astype(jnp.bfloat16),
        value_acc.astype(jnp.bfloat16),
    )


def push_mix(numerators, gradient, push_weights, out_links, denominators):
    rep_count = lax.axis_size("rep")
    own_index = lax.axis_index("rep")
    sources = jnp.arange(rep_count)
    link_row = jnp.sum(
        jnp.where(sources[:, None] == own_index, out_links, jnp.zeros_like(out_links)), axis=0
    )
    den_own = pick_entry(denominators, own_index).astype(jnp.float32)
    kept_share = 1.0 - jnp.sum(link_row).astype(jnp.float32) / den_own
    half_step = numerators[0].astype(jnp.float32) - step_size * gradient
    sending = (half_step / den_own).astype(jnp.bfloat16)
    mixed_sum = kept_share * half_step
    for bit_level in range(rep_count.bit_length() - 1):
        offset = 1 << bit_level
        linked = pick_entry(link_row, (own_index + offset) % rep_count)
        outgoing = jnp.where(linked > 0, sending, jnp.zeros_like(sending))
        mixed_sum = mixed_sum + shifted(outgoing, "rep", offset).astype(jnp.float32)
    own_weight = push_weights[0]
    share_vector = link_row.astype(jnp.float32) * (own_weight / den_own) + jnp.where(
        sources == own_index, kept_share * own_weight, 0.0
    )
    weight_totals = lax.psum(share_vector, "rep")
    new_weight = pick_entry(weight_totals, own_index)
    return (mixed_sum.astype(jnp.bfloat16)[None], new_weight[None])


def body(
    queries,
    key_rows,
    value_rows,
    cotangent,
    numerators,
    push_weights,
    doc_ids,
    out_links,
    denominators,
):
    head_q, head_k, head_v = (
        lax.all_to_all(queries, "seq", split_axis=2, concat_axis=1, tiled=True),
        lax.all_to_all(key_rows, "seq", split_axis=2, concat_axis=1, tiled=True),
        lax.all_to_all(value_rows, "seq", split_axis=2, concat_axis=1, tiled=True),
    )
    seq_len = head_q.shape[1]
    local_width = head_q.shape[2]
    head_count = local_width // HEAD_DIM
    query_heads = head_q[0].reshape(seq_len, head_count, HEAD_DIM)
    key_heads = head_k[0].reshape(seq_len, head_count, HEAD_DIM)
    value_heads = head_v[0].reshape(seq_len, head_count, HEAD_DIM)
    prob_blocks, attended = attend_forward(query_heads, key_heads, value_heads, doc_ids[0])
    attended_flat = attended.reshape(seq_len, local_width)
    debiased = (numerators[0].astype(jnp.float32) / push_weights[0]).astype(jnp.bfloat16)
    gathered = lax.all_gather(cotangent, "seq", axis=1, tiled=True)[0]
    gradient = lax.dot_general(
        attended_flat, gathered, (((0,), (0,)), ((), ())), preferred_element_type=jnp.float32
    )
    grad_attn = lax.dot_general(
        gathered, debiased, (((1,), (1,)), ((), ())), preferred_element_type=jnp.float32
    ).astype(jnp.bfloat16)
    grad_heads = grad_attn.reshape(seq_len, head_count, HEAD_DIM)
    query_grad, key_grad, value_grad = attend_backward(
        query_heads, key_heads, value_heads, prob_blocks, attended, grad_heads
    )
    mixed, new_weight = push_mix(numerators, gradient, push_weights, out_links, denominators)
    back_q, back_k, back_v = (
        lax.all_to_all(
            query_grad.reshape(1, seq_len, local_width),
            "seq",
            split_axis=1,
            concat_axis=2,
            tiled=True,
        ),
        lax.all_to_all(
            key_grad.reshape(1, seq_len, local_width),
            "seq",
            split_axis=1,
            concat_axis=2,
            tiled=True,
        ),
        lax.all_to_all(
            value_grad.reshape(1, seq_len, local_width),
            "seq",
            split_axis=1,
            concat_axis=2,
            tiled=True,
        ),
    )
    return (back_q, back_k, back_v, mixed, new_weight)


def solution(mesh):
    placed = (
        P("rep", "seq", None),
        P("rep", "seq", None),
        P("rep", "seq", None),
        P("rep", "seq", None),
        P("rep", "seq", None),
        P("rep"),
        P("rep", None),
        P(),
        P(),
    )
    return jax.shard_map(
        body,
        mesh=mesh,
        in_specs=placed,
        out_specs=(
            P("rep", "seq", None),
            P("rep", "seq", None),
            P("rep", "seq", None),
            P("rep", "seq", None),
            P("rep"),
        ),
        check_vma=False,
    )
```

profile of v0, /device:TPU:12, one launch (start us, length us, event | category | flops | bytes accessed | tf_op | source)
XLA Modules:
  0.0 574.6 jit_solution(15662956200618608234)
XLA Ops:
  7.9 5.0 copy.258
  13.5 22.4 %reduce.28 = bf16[4096,128]{1,0:T(8,128)(2,1)S(1)} reduce(bf16[4096,1,128]{2,1,0:T(2,128)(2,1)S(1)} %bitcast.239, bf16[]{:T(256)} %broadcast.376), dimensions={1}, to_apply=%bitcast.163.reduce_sub_computation | reduce | bytes 2097154
  37.0 8.6 %all-to-all-start.1 = ((bf16[16,2,16384]{2,1,0:T(2,128)(2,1)}), bf16[16,2,16384]{2,1,0:T(2,128)(2,1)S(1)}, u32[]{:S(2)}, u32[]{:S(2)}) async-start(bf16[16,2,16384]{2,1,0:T(2,128)(2,1)} %reshape.556), calls=%async_computation.1 | async-start | bytes 2097152 | tf_op jit(solution)/shard_map/all_to_all | solution.py:156
  45.5 5.1 copy.262
  50.6 23.4 %reduce.29 = bf16[4096,128]{1,0:T(8,128)(2,1)} reduce(bf16[4096,1,128]{2,1,0:T(2,128)(2,1)S(1)} %bitcast.243, bf16[]{:T(256)} %broadcast.376), dimensions={1}, to_apply=%bitcast.165.reduce_sub_computation | reduce | bytes 2097154
  76.2 6.9 %all-to-all-done.1 = bf16[16,2,16384]{2,1,0:T(2,128)(2,1)S(1)} async-done(((bf16[16,2,16384]{2,1,0:T(2,128)(2,1)}), bf16[16,2,16384]{2,1,0:T(2,128)(2,1)S(1)}, u32[]{:S(2)}, u32[]{:S(2)}) %all-to-all-start.1) | async-done | bytes 1048608 | tf_op jit(solution)/shard_map/all_to_all | solution.py:156
  83.0 15.8 %all-to-all-start.2 = ((bf16[16,2,16384]{2,1,0:T(2,128)(2,1)}), bf16[16,2,16384]{2,1,0:T(2,128)(2,1)}, u32[]{:S(2)}, u32[]{:S(2)}) async-start(bf16[16,2,16384]{2,1,0:T(2,128)(2,1)} %reshape.558), calls=%async_computation.2 | async-start | bytes 2097152 | tf_op jit(solution)/shard_map/all_to_all | solution.py:157
  104.8 5.0 copy.256
  109.9 23.4 %reduce.27 = bf16[4096,128]{1,0:T(8,128)(2,1)} reduce(bf16[4096,1,128]{2,1,0:T(2,128)(2,1)S(1)} %bitcast.244, bf16[]{:T(256)} %broadcast.376), dimensions={1}, to_apply=%bitcast.161.reduce_sub_computation | reduce | bytes 2097154
  136.3 6.5 %all-to-all-start = ((bf16[16,2,16384]{2,1,0:T(2,128)(2,1)}), bf16[16,2,16384]{2,1,0:T(2,128)(2,1)}, u32[]{:S(2)}, u32[]{:S(2)}) async-start(bf16[16,2,16384]{2,1,0:T(2,128)(2,1)} %reshape.554), calls=%async_computation | async-start | bytes 2097152 | tf_op jit(solution)/shard_map/all_to_all | solution.py:155
  154.1 4.3 reshape.559
  161.7 7.8 %all-to-all-done = bf16[16,2,16384]{2,1,0:T(2,128)(2,1)} async-done(((bf16[16,2,16384]{2,1,0:T(2,128)(2,1)}), bf16[16,2,16384]{2,1,0:T(2,128)(2,1)}, u32[]{:S(2)}, u32[]{:S(2)}) %all-to-all-start) | async-done | bytes 1048608 | tf_op jit(solution)/shard_map/all_to_all | solution.py:155
  169.5 4.3 reshape.555
  192.7 4.8 fusion.111
  197.6 6.4 %fusion.108 = (f32[2,512]{1,0:T(2,128)S(1)}, f32[2,512,1536]{2,1,0:T(8,128)}) fusion(pred[512,1536]{1,0:T(8,128)(4,1)} %compare_and_fusion, bf16[512,2,128]{0,2,1:T(8,128)(2,1)S(1)} %reshape.552, bf16[1536,2,128]{2,1,0:T(2,128)(2,1)S(1)} %copy-done.43), kind=kOutput, calls=%fused_computation.154 | convolution fusion | flops 408946176 | bytes 8130560 | tf_op jit(solution)/shard_map/sub | solution.py:52
  204.0 5.6 fusion.107
  209.6 4.2 divide_convert_fusion.2
  220.3 9.7 %fusion.38 = bf16[2048,256]{0,1:T(8,128)(2,1)S(1)} fusion(bf16[1,2048,3584]{2,1,0:T(8,128)(2,1)} %all-gather.2.cloned.1.call-done, bf16[1,256,3584]{2,1,0:T(8,128)(2,1)} %param.33, f32[]{:T(128)} %bitcast.220), kind=kOutput, calls=%fused_computation.54 | convolution fusion | flops 3761373184 | bytes 17563652 | tf_op jit(solution)/shard_map/dot_general | solution.py:172
  258.6 3.4 multiply_convert_fusion
  263.7 11.6 %reduce.32 = bf16[2048,256]{1,0:T(8,128)(2,1)} reduce(bf16[2048,1,256]{2,1,0:T(2,128)(2,1)S(1)} %bitcast.241, bf16[]{:T(256)} %broadcast.376), dimensions={1}, to_apply=%bitcast.171.reduce_sub_computation | reduce | bytes 2097154
  277.6 4.8 all-to-all-start.5
  294.2 4.6 copy.311
  298.8 11.6 %reduce.31 = bf16[2048,256]{1,0:T(8,128)(2,1)} reduce(bf16[2048,1,256]{2,1,0:T(2,128)(2,1)S(1)} %bitcast.242, bf16[]{:T(256)} %broadcast.376), dimensions={1}, to_apply=%bitcast.169.reduce_sub_computation | reduce | bytes 2097154
  312.6 12.5 %broadcast_select_fusion.3 = (bf16[256,3584]{1,0:T(8,128)(2,1)}, bf16[256,3584]{1,0:T(8,128)(2,1)S(1)}, f32[256,3584]{1,0:T(8,128)}) fusion(pred[]{:T(512)S(6)} %gt.12, f32[]{:T(128)S(6)} %convert_element_type.175, bf16[2048,256]{0,1:T(8,128)(2,1)} %bitcast.267, bf16[1,2048,3584]{2,1,0:T(8,128)(2,1)} %all-gather.2.cloned.1.call-done, ...), kind=kOutput, calls=%fused_computation.70 | convolution fusion | flops 3763601408 | bytes 24903684 | tf_op jit(solution)/shard_map/dot_general | solution.py:169
  326.6 7.3 %all-to-all-start.4 = ((bf16[16,2,16384]{2,1,0:T(2,128)(2,1)}), bf16[16,2,16384]{2,1,0:T(2,128)(2,1)}, u32[]{:S(2)}, u32[]{:S(2)}) async-start(bf16[16,2,16384]{2,1,0:T(2,128)(2,1)} %reshape.562), calls=%async_computation.4 | async-start | bytes 2097152 | tf_op jit(solution)/shard_map/all_to_all | solution.py:188
  346.9 4.6 copy.299
  351.5 11.6 %reduce.30 = bf16[2048,256]{1,0:T(8,128)(2,1)} reduce(bf16[2048,1,256]{2,1,0:T(2,128)(2,1)S(1)} %bitcast.240, bf16[]{:T(256)} %broadcast.376), dimensions={1}, to_apply=%bitcast.167.reduce_sub_computation | reduce | bytes 2097154
  365.3 7.2 %all-to-all-start.3 = ((bf16[16,2,16384]{2,1,0:T(2,128)(2,1)}), bf16[16,2,16384]{2,1,0:T(2,128)(2,1)}, u32[]{:S(2)}, u32[]{:S(2)}) async-start(bf16[16,2,16384]{2,1,0:T(2,128)(2,1)} %reshape.560), calls=%async_computation.3 | async-start | bytes 2097152 | tf_op jit(solution)/shard_map/all_to_all | solution.py:181
  373.1 170.7 %psum.7 = f32[16]{0:T(128)S(1)} all-reduce(f32[16]{0:T(128)S(1)} %select_add_fusion), channel_id=1, replica_groups=mesh['rep'=16,'seq'=16] {'rep'}, use_global_device_ids=true, to_apply=%region_15.16 | all-reduce | flops 16 | bytes 128 | tf_op jit(solution)/shard_map/psum | solution.py:138
  544.5 6.7 %fusion.45 = bf16[1,256,3584]{2,1,0:T(8,128)(2,1)} fusion(bf16[256,3584]{1,0:T(8,128)(2,1)} %collective-permute-done.3, bf16[256,3584]{1,0:T(8,128)(2,1)} %collective-permute-done.2, bf16[256,3584]{1,0:T(8,128)(2,1)} %collective-permute-done.1, bf16[256,3584]{1,0:T(8,128)(2,1)} %collective-permute-done, f32[256,3584]{1,0:T(8,128)} %get-tuple-element.176, ...), kind=kLoop, calls=%fused_computation.64 | loop fusion | flops 9175040 | bytes 12845060 | tf_op jit(solution)/shard_map/broadcast_in_dim | solution.py:140
  554.3 4.3 reshape.563
  560.8 4.3 reshape.561
  (233 shorter events, 120.5 us)
Async XLA Ops:
  7.2 213.1 %all-gather.2.cloned.1.call-start = ((), (), s32[]{:S(2)}) async-start(), calls=%async_computation.6 | async-start | bytes 15597568 | tf_op jit(solution)/shard_map/all_gather | solution.py:168
  37.0 46.1 %all-to-all-start.1 = ((bf16[16,2,16384]{2,1,0:T(2,128)(2,1)}), bf16[16,2,16384]{2,1,0:T(2,128)(2,1)S(1)}, u32[]{:S(2)}, u32[]{:S(2)}) async-start(bf16[16,2,16384]{2,1,0:T(2,128)(2,1)} %reshape.556), calls=%async_computation.1 | async-start | bytes 2097152 | tf_op jit(solution)/shard_map/all_to_all | solution.py:156
  74.0 25.5 %copy-start.51 = (s32[16]{0:T(128)S(1)}, s32[16]{0:T(128)}, u32[]{:S(2)}) copy-start(s32[16]{0:T(128)} %param.37) | copy-start | bytes 196
  74.0 26.9 %copy-start.50 = (s32[16,16]{1,0:T(8,128)S(1)}, s32[16,16]{1,0:T(8,128)}, u32[]{:S(2)}) copy-start(s32[16,16]{1,0:T(8,128)} %param.36) | copy-start | bytes 3076
  83.0 53.3 %all-to-all-start.2 = ((bf16[16,2,16384]{2,1,0:T(2,128)(2,1)}), bf16[16,2,16384]{2,1,0:T(2,128)(2,1)}, u32[]{:S(2)}, u32[]{:S(2)}) async-start(bf16[16,2,16384]{2,1,0:T(2,128)(2,1)} %reshape.558), calls=%async_computation.2 | async-start | bytes 2097152 | tf_op jit(solution)/shard_map/all_to_all | solution.py:157
  133.2 9.6 %copy-start.49 = (s32[1,2048]{1,0:T(1,128)S(1)}, s32[1,2048]{1,0:T(1,128)}, u32[]{:S(2)}) copy-start(s32[1,2048]{1,0:T(1,128)} %param.35) | copy-start | bytes 24580
  133.2 10.6 %slice-start.2 = ((s32[1,2048]{1,0:T(1,128)}), s32[1,1024]{1,0:T(1,128)S(1)}, s32[]{:S(2)}) async-start(s32[1,2048]{1,0:T(1,128)} %param.35), calls=%async_computation.9 | async-start | bytes 8192 | tf_op jit(solution)/shard_map/slice | solution.py:48
  136.3 33.2 %all-to-all-start = ((bf16[16,2,16384]{2,1,0:T(2,128)(2,1)}), bf16[16,2,16384]{2,1,0:T(2,128)(2,1)}, u32[]{:S(2)}, u32[]{:S(2)}) async-start(bf16[16,2,16384]{2,1,0:T(2,128)(2,1)} %reshape.554), calls=%async_computation | async-start | bytes 2097152 | tf_op jit(solution)/shard_map/all_to_all | solution.py:155
  176.4 21.1 %copy-start.25 = (bf16[512,2,128]{0,2,1:T(8,128)(2,1)}, bf16[512,2,128]{0,2,1:T(8,128)(2,1)S(1)}, u32[]{:S(2)}) copy-start(bf16[512,2,128]{0,2,1:T(8,128)(2,1)S(1)} %reshape.552) | copy-start | bytes 786436
  176.4 6.3 %copy-start.14 = (bf16[1,16,128,256]{2,1,3,0:T(8,128)(2,1)S(1)}, bf16[1,16,128,256]{2,1,3,0:T(8,128)(2,1)}, u32[]{:S(2)}) copy-start(bf16[1,16,128,256]{2,1,3,0:T(8,128)(2,1)} %copy.290) | copy-start | bytes 3145732
  178.4 5.6 copy-start.19
  192.7 4.8 copy-start.43
  197.6 6.4 %copy-start.31 = (bf16[2048,2,128]{0,2,1:T(8,128)(2,1)S(1)}, bf16[2048,2,128]{0,2,1:T(8,128)(2,1)}, u32[]{:S(2)}) copy-start(bf16[2048,2,128]{0,2,1:T(8,128)(2,1)} %reshape_squeeze.7) | copy-start | bytes 3145732
  197.6 6.4 %copy-start.33 = (pred[512,2048]{1,0:T(8,128)(4,1)S(1)}, pred[512,2048]{1,0:T(8,128)(4,1)}, u32[]{:S(2)}) copy-start(pred[512,2048]{1,0:T(8,128)(4,1)} %fusion.18) | copy-start | bytes 3145732
  197.6 6.4 %copy-start.41 = (bf16[512,2,128]{0,2,1:T(8,128)(2,1)S(1)}, bf16[512,2,128]{0,2,1:T(8,128)(2,1)}, u32[]{:S(2)}) copy-start(bf16[512,2,128]{0,2,1:T(8,128)(2,1)} %reshape.553) | copy-start | bytes 786436
  209.5 4.5 copy-start.13
  209.6 6.0 %slice-start = ((s8[8388608]{0:T(1024)(128)(4,1)}), s8[4194304]{0:T(1024)(128)(4,1)S(1)}, s32[]{:S(2)}) async-start(s8[8388608]{0:T(1024)(128)(4,1)} %bitcast.237), calls=%async_computation.7 | async-start | bytes 8388608
  275.3 7.2 %copy-start.1 = (f32[2048,2,128]{2,0,1:T(8,128)S(1)}, f32[2048,2,128]{2,0,1:T(8,128)}, u32[]{:S(2)}) copy-start(f32[2048,2,128]{2,0,1:T(8,128)} %scatter-add.20) | copy-start | bytes 6291460
  275.3 7.2 %copy-start.28 = (bf16[512,2,128]{0,2,1:T(8,128)(2,1)S(1)}, bf16[512,2,128]{0,2,1:T(8,128)(2,1)}, u32[]{:S(2)}) copy-start(bf16[512,2,128]{0,2,1:T(8,128)(2,1)} %reshape.551) | copy-start | bytes 786436
  277.6 49.0 %all-to-all-start.5 = ((bf16[16,2,16384]{2,1,0:T(2,128)(2,1)}), bf16[16,2,16384]{2,1,0:T(2,128)(2,1)S(1)}, u32[]{:S(2)}, u32[]{:S(2)}) async-start(bf16[16,2,16384]{2,1,0:T(2,128)(2,1)} %reshape.564), calls=%async_computation.5 | async-start | bytes 2097152 | tf_op jit(solution)/shard_map/all_to_all | solution.py:195
  325.0 219.4 %collective-permute-start = (bf16[256,3584]{1,0:T(8,128)(2,1)}, bf16[256,3584]{1,0:T(8,128)(2,1)}, u32[]{:S(2)}, u32[]{:S(2)}) collective-permute-start(bf16[256,3584]{1,0:T(8,128)(2,1)} %get-tuple-element.143), channel_id=1, source_target_pairs={{0,16},{16,32},{32,48},{48,64},{64,80},{80,96},{96,112},{112,128},... | collective-permute-start | bytes 5505032 | tf_op jit(solution)/shard_map/ppermute | solution.py:16
  326.6 38.6 %all-to-all-start.4 = ((bf16[16,2,16384]{2,1,0:T(2,128)(2,1)}), bf16[16,2,16384]{2,1,0:T(2,128)(2,1)}, u32[]{:S(2)}, u32[]{:S(2)}) async-start(bf16[16,2,16384]{2,1,0:T(2,128)(2,1)} %reshape.562), calls=%async_computation.4 | async-start | bytes 2097152 | tf_op jit(solution)/shard_map/all_to_all | solution.py:188
  333.9 6.8 %copy-start.11 = (bf16[2,512,1024]{2,1,0:T(8,128)(2,1)S(1)}, bf16[2,512,1024]{2,1,0:T(8,128)(2,1)}, u32[]{:S(2)}) copy-start(bf16[2,512,1024]{2,1,0:T(8,128)(2,1)} %multiply_convert_fusion.2) | copy-start | bytes 6291460
  333.9 6.8 %copy-start.46 = (bf16[1024,2,128]{0,2,1:T(8,128)(2,1)S(1)}, bf16[1024,2,128]{0,2,1:T(8,128)(2,1)}, u32[]{:S(2)}) copy-start(bf16[1024,2,128]{0,2,1:T(8,128)(2,1)} %slice.339) | copy-start | bytes 1572868
  333.9 8.1 %copy-start.44 = (bf16[1536,2,128]{2,1,0:T(2,128)(2,1)S(1)}, bf16[1536,2,128]{2,1,0:T(2,128)(2,1)}, u32[]{:S(2)}) copy-start(bf16[1536,2,128]{2,1,0:T(2,128)(2,1)} %slice.352) | copy-start | bytes 2359300
  333.9 9.1 %copy-start.32 = (bf16[2048,2,128]{0,2,1:T(8,128)(2,1)S(1)}, bf16[2048,2,128]{0,2,1:T(8,128)(2,1)}, u32[]{:S(2)}) copy-start(bf16[2048,2,128]{0,2,1:T(8,128)(2,1)} %reshape_squeeze.7) | copy-start | bytes 3145732
  336.9 4.6 copy-start.9
  336.9 4.6 copy-start.37
  336.9 207.6 %collective-permute-start.1 = (bf16[256,3584]{1,0:T(8,128)(2,1)}, bf16[256,3584]{1,0:T(8,128)(2,1)}, u32[]{:S(2)}, u32[]{:S(2)}) collective-permute-start(bf16[256,3584]{1,0:T(8,128)(2,1)} %get-tuple-element.145), channel_id=1, source_target_pairs={{0,32},{16,48},{32,64},{48,80},{64,96},{80,112},{96,128},{112,144}... | collective-permute-start | bytes 5505032 | tf_op jit(solution)/shard_map/ppermute | solution.py:16
  338.4 206.0 %collective-permute-start.2 = (bf16[256,3584]{1,0:T(8,128)(2,1)}, bf16[256,3584]{1,0:T(8,128)(2,1)}, u32[]{:S(2)}, u32[]{:S(2)}) collective-permute-start(bf16[256,3584]{1,0:T(8,128)(2,1)} %get-tuple-element.146), channel_id=1, source_target_pairs={{0,64},{16,80},{32,96},{48,112},{64,128},{80,144},{96,160},{112,17... | collective-permute-start | bytes 5505032 | tf_op jit(solution)/shard_map/ppermute | solution.py:16
  338.9 205.5 %collective-permute-start.3 = (bf16[256,3584]{1,0:T(8,128)(2,1)}, bf16[256,3584]{1,0:T(8,128)(2,1)}, u32[]{:S(2)}, u32[]{:S(2)}) collective-permute-start(bf16[256,3584]{1,0:T(8,128)(2,1)} %get-tuple-element.147), channel_id=1, source_target_pairs={{0,128},{16,144},{32,160},{48,176},{64,192},{80,208},{96,224},{112... | collective-permute-start | bytes 5505032 | tf_op jit(solution)/shard_map/ppermute | solution.py:16
  365.3 195.6 %all-to-all-start.3 = ((bf16[16,2,16384]{2,1,0:T(2,128)(2,1)}), bf16[16,2,16384]{2,1,0:T(2,128)(2,1)}, u32[]{:S(2)}, u32[]{:S(2)}) async-start(bf16[16,2,16384]{2,1,0:T(2,128)(2,1)} %reshape.560), calls=%async_computation.3 | async-start | bytes 2097152 | tf_op jit(solution)/shard_map/all_to_all | solution.py:181
  (34 other events, 78.8 us)
Sparse Core Ops, SparseCore 0:
  9.8 133.2 all-gather.1
where the time goes:
time: 584 us; the launch traced here: 575 us
  blocking collectives  171 us (29%)
  other arithmetic  132 us (23%)
  local copies, waits for them, and re-layouts  108 us (18%)
  matrix products  72.3 us (12%)
  starting transfers between devices  55.6 us (10%)
  between operations  20 us (3%)
  waiting for transfers between devices  16.3 us (3%)
    psum x1, blocking collectives, push_mix(): weight_totals = lax.psum(share_vector, 'rep')  171 us
    unnamed x7, other arithmetic  104 us
    unnamed x137, local copies, waits for them, and re-layouts  63.8 us
    sub x4, matrix products, attend_forward(): exponent = jnp.exp(scores - row_peak)  17.7 us
    all_to_all x1, starting transfers between devices, body(): lax.all_to_all(value_rows, 'seq', split_axis=2, concat_axis=1, tiled=True)  15.8 us
    dot_general x1, matrix products, body(): lax.dot_general(attended_flat, gathered, (((0,), (0,)), ((), ())), prefer...  12.5 us
  transfers between devices with their start and end apart: 11, of which 3 were waited for; matrix products, arithmetic and copies ran while one was open for 43% of the time, Pallas kernels for 0%

commit v1 on v0

v1 whole, which is shorter than its diff:
```python
import math

import jax
import jax.numpy as jnp
from jax import lax
from jax.experimental import pallas as pl
from jax.experimental.pallas import tpu as pltpu
from jax.sharding import PartitionSpec as P

HD = 128
SEQ = 2048
TOK = 128
OUTW = 3584
FW = 256
REACH = 4
WIN = REACH + 1
PAD = REACH * 256
CH = 256
NCH = OUTW // CH
STEP_SIZE = 3.0
SCALE = 1.0 / math.sqrt(HD)
EXP2_SCALE = SCALE * math.log2(math.e)
NEG = -1e30
MESH = pl.DeviceIdType.MESH
BF = jnp.bfloat16
F32 = jnp.float32


def mod(a, n):
    return lax.rem(a, n)


def dot_nn(a, b):
    return lax.dot_general(a, b, (((1,), (0,)), ((), ())), preferred_element_type=F32)


def dot_nt(a, b):
    return lax.dot_general(a, b, (((1,), (1,)), ((), ())), preferred_element_type=F32)


def rows(start, size):
    return pl.ds(pl.multiple_of(start, size), size)


def kernel(
    q_ref, k_ref, v_ref, cot_ref, num_ref, doc_ref, pw_ref, links_ref, den_ref,
    dq_out, dk_out, dv_out, mix_out, w_out,
    qh, kp, vp, kt, vt, pb, sbuf, ot, cotb, numb, deb, acc, dqb, dkb, dvb, dcol,
    rb, mixb, wsend, wrecv,
    loc_sem, in_send, in_recv, ring_send, ring_recv, sib_send, sib_recv,
    out_send, out_recv, push_send, push_recv, wp_send, wp_recv, mix_sem,
):
    rep = lax.axis_index("rep")
    me = lax.axis_index("seq")
    x, y = lax.div(rep, 4), mod(rep, 4)
    z, core = lax.div(me, 2), mod(me, 2)
    way = 1 - 2 * core
    sibling = (rep, z * 2 + 1 - core)
    ring_next = (rep, mod(z + way + 8, 8) * 2 + core)

    def at_xy(dx, dy):
        return (mod(x + dx + 4, 4) * 4 + mod(y + dy + 4, 4), me)

    push_to = (at_xy(0, 1), at_xy(0, 2), at_xy(2, 0), at_xy(1, 0))

    barrier = pltpu.get_barrier_semaphore()
    for step in range(1, 16):
        pl.semaphore_signal(
            barrier, inc=1, device_id=(rep, mod(me + step, 16)), device_id_type=MESH
        )
    for dx, dy in ((0, 1), (0, 2), (0, 3), (1, 0), (2, 0), (3, 0)):
        pl.semaphore_signal(barrier, inc=1, device_id=at_xy(dx, dy), device_id_type=MESH)
    pl.semaphore_wait(barrier, 21)

    def remote(src, dst, send, recv, device):
        return pltpu.make_async_remote_copy(
            src_ref=src, dst_ref=dst, send_sem=send, recv_sem=recv, device_id=device,
            device_id_type=MESH,
        )

    heads_in = ((q_ref, qh, 0), (k_ref, kp, PAD), (v_ref, vp, PAD))

    def in_copy(t, dst, src):
        source, target, base = heads_in[t]
        return remote(
            source.at[:, rows(dst * FW, FW)],
            target.at[pl.ds(pl.multiple_of(base + src * TOK, TOK), TOK), :],
            in_send.at[t, dst], in_recv.at[t, src], (rep, dst),
        )

    def in_own(t):
        source, target, base = heads_in[t]
        return pltpu.make_async_copy(
            source.at[:, rows(me * FW, FW)],
            target.at[pl.ds(pl.multiple_of(base + me * TOK, TOK), TOK), :],
            loc_sem.at[t],
        )

    own_cot = pltpu.make_async_copy(cot_ref, cotb.at[rows(me * TOK, TOK), :], loc_sem.at[3])
    own_num = pltpu.make_async_copy(num_ref, numb, loc_sem.at[4])

    def send_in(step, carry):
        dst = mod(me + step, 16)
        for t in range(3):
            in_copy(t, dst, me).start()
        return carry

    own_num.start()
    own_cot.start()
    lax.fori_loop(1, 16, send_in, 0)
    for t in range(3):
        in_own(t).start()

    def ring_block(step):
        return mod(z - way * step + 8, 8) * 2 + core

    def sib_block(step):
        return mod(z + way * step + 8, 8) * 2 + 1 - core

    def half_rows(block, sub):
        return cotb.at[pl.ds(pl.multiple_of(block * TOK + sub * 64, 64), 64), :]

    def ring_copy(step, sub):
        piece = half_rows(ring_block(step), sub)
        return remote(piece, piece, ring_send.at[step, sub], ring_recv.at[step + 1, sub], ring_next)

    def ring_arrival(step, sub):
        piece = half_rows(ring_block(step), sub)
        return remote(piece, piece, ring_send.at[step, sub], ring_recv.at[step, sub], ring_next)

    def sib_copy(step, sub):
        piece = half_rows(ring_block(step), sub)
        return remote(piece, piece, sib_send.at[step, sub], sib_recv.at[step, sub], sibling)

    def sib_arrival(step, sub):
        piece = half_rows(sib_block(step), sub)
        return remote(piece, piece, sib_send.at[step, sub], sib_recv.at[step, sub], sibling)

    own_cot.wait()
    for sub in range(2):
        ring_copy(0, sub).start()
        sib_copy(0, sub).start()

    kp[0:PAD, :] = jnp.zeros((PAD, FW), BF)
    vp[0:PAD, :] = jnp.zeros((PAD, FW), BF)
    dcol[0:PAD, :] = jnp.full((PAD, 128), -1.0, F32)

    def zero_acc(i, carry):
        acc[rows(i * 256, 256), :] = jnp.zeros((256, FW), F32)
        return carry

    lax.fori_loop(0, acc.shape[0] // 256, zero_acc, 0)

    def doc_columns(i, carry):
        part = doc_ref[:, rows(i * 128, 128)].astype(F32)
        dcol[pl.ds(pl.multiple_of(PAD + i * 128, 128), 128), :] = jnp.broadcast_to(
            part, (128, 128)
        ).T
        return carry

    lax.fori_loop(0, SEQ // 128, doc_columns, 0)
    own_num.wait()
    inv_weight = 1.0 / jnp.full((1, CH), pw_ref[0], F32)

    def debias(j, carry):
        cols = rows(j * CH, CH)
        deb[:, cols] = (numb[:, cols].astype(F32) * inv_weight).astype(BF)
        return carry

    lax.fori_loop(0, NCH, debias, 0)

    def wait_in(step, carry):
        src = mod(me - step + 16, 16)
        for t in range(3):
            in_copy(t, mod(me + step, 16), src).wait_recv()
        return carry

    for t in range(3):
        in_own(t).wait()
    lax.fori_loop(1, 16, wait_in, 0)

    def flip(i, carry):
        cols = rows(i * 256, 256)
        kt[:, cols] = kp[cols, :].T
        vt[:, cols] = vp[cols, :].T
        return carry

    lax.fori_loop(0, (PAD + SEQ) // 256, flip, 0)

    later_key = lax.broadcasted_iota(jnp.int32, (256, 256), 0) <= lax.broadcasted_iota(
        jnp.int32, (256, 256), 1
    )

    def forward(a):
        doc_q = doc_ref[:, rows(a * 256, 256)].astype(F32)
        for h in range(2):
            feats = slice(h * HD, (h + 1) * HD)
            qa = qh[rows(a * 256, 256), feats]
            peak = jnp.full((1, 256), NEG, F32)
            for c in range(WIN):
                keys = rows((a + c) * 256, 256)
                scores = dot_nt(kp[keys, feats], qa)
                dk_col = dcol[keys, :]
                allowed = jnp.concatenate([dk_col, dk_col], axis=1) == doc_q
                if c == REACH:
                    allowed = allowed & later_key
                scores = jnp.where(allowed, scores, NEG)
                sbuf[h, c * 256:(c + 1) * 256, :] = scores
                peak = jnp.maximum(peak, jnp.max(scores, axis=0, keepdims=True))
            total = jnp.zeros((1, 256), F32)
            for c in range(WIN):
                part = slice(c * 256, (c + 1) * 256)
                expo = jnp.exp2((sbuf[h, part, :] - peak) * EXP2_SCALE)
                sbuf[h, part, :] = expo
                total = total + jnp.sum(expo, axis=0, keepdims=True)
            inv_total = 1.0 / total
            out = jnp.zeros((HD, 256), F32)
            for c in range(WIN):
                probs = (sbuf[h, c * 256:(c + 1) * 256, :] * inv_total).astype(BF)
                pb[rows(((a * 2 + h) * WIN + c) * 256, 256), :] = probs
                out = out + dot_nn(vt[feats, rows((a + c) * 256, 256)], probs)
            ot[feats, rows(a * 256, 256)] = out.astype(BF)

    def out_copy(t, dst, src):
        source, target = ((dqb, dq_out), (dkb, dk_out), (dvb, dv_out))[t]
        return remote(
            source.at[rows(dst * TOK, TOK), :], target.at[:, rows(src * FW, FW)],
            out_send.at[t, dst], out_recv.at[t, src], (rep, dst),
        )

    def out_own(t):
        source, target = ((dqb, dq_out), (dkb, dk_out), (dvb, dv_out))[t]
        return pltpu.make_async_copy(
            source.at[rows(me * TOK, TOK), :], target.at[:, rows(me * FW, FW)], loc_sem.at[5 + t]
        )

    def backward(a, half):
        device = a * 2 + half
        tok = rows(device * TOK, TOK)
        lanes = slice(half * TOK, (half + 1) * TOK)
        grad = dot_nt(deb[...], cotb[tok, :]).astype(BF)
        for h in range(2):
            feats = slice(h * HD, (h + 1) * HD)
            go = grad[feats, :]
            centre = jnp.sum(
                go.astype(F32) * ot[feats, tok].astype(F32), axis=0, keepdims=True
            )
            qa = qh[tok, feats]
            dq = jnp.zeros((HD, TOK), F32)
            for c in range(WIN):
                keys = rows((a + c) * 256, 256)
                probs = pb[rows(((a * 2 + h) * WIN + c) * 256, 256), lanes]
                grad_probs = dot_nn(vp[keys, feats], go)
                grad_scores = (probs.astype(F32) * (grad_probs - centre)).astype(BF)
                k_rows = keys
                v_rows = pl.ds(pl.multiple_of(PAD + SEQ + (a + c) * 256, 256), 256)
                acc[k_rows, feats] += dot_nn(grad_scores, qa)
                acc[v_rows, feats] += dot_nt(probs, go)
                dq = dq + dot_nn(kt[feats, keys], grad_scores)
            dqb[tok, feats] = (dq * SCALE).T.astype(BF)

        @pl.when(device != me)
        def _():
            out_copy(0, device, me).start()

        @pl.when(device == me)
        def _():
            out_own(0).start()

    def ring_step(s, carry):
        before = mod(z - s + 8, 8)
        after = mod(z + s, 8)

        def take(sub):
            @pl.when(s > 0)
            def _():
                ring_arrival(s, sub).wait_recv()

                @pl.when(s < 7)
                def _():
                    ring_copy(s, sub).start()

                sib_copy(s, sub).start()

        take(0)

        @pl.when(s <= 4)
        def _():
            forward(before)

        take(1)

        @pl.when((s >= 1) & (s <= 3))
        def _():
            forward(after)

        for sub in range(2):
            sib_arrival(s, sub).wait_recv()
        backward(before, 0)
        backward(after, 1)
        return carry

    lax.fori_loop(0, 8, ring_step, 0)

    def finish(i, carry):
        dst = mod(me + i, 16)
        tok = rows(dst * TOK, TOK)
        dkb[tok, :] = (
            acc[pl.ds(pl.multiple_of(PAD + dst * TOK, TOK), TOK), :] * SCALE
        ).astype(BF)
        dvb[tok, :] = acc[
            pl.ds(pl.multiple_of(2 * PAD + SEQ + dst * TOK, TOK), TOK), :
        ].astype(BF)

        @pl.when(i > 0)
        def _():
            out_copy(1, dst, me).start()
            out_copy(2, dst, me).start()

        @pl.when(i == 0)
        def _():
            out_own(1).start()
            out_own(2).start()

        return carry

    lax.fori_loop(0, 16, finish, 0)

    link = [links_ref[rep, mod(rep + off, 16)].astype(F32) for off in (1, 2, 8, 4)]
    inv_den = 1.0 / jnp.full((1, CH), den_ref[rep].astype(F32), F32)
    links_out = links_ref[rep, 0]
    for col in range(1, 16):
        links_out = links_out + links_ref[rep, col]
    kept = 1.0 - jnp.full((1, CH), links_out.astype(F32), F32) * inv_den
    from_1 = jnp.where(y >= 1, 1.0, 0.0)
    from_2 = jnp.where(y >= 2, 1.0, 0.0)
    carry_1 = jnp.where(y == 0, 1.0, 0.0)
    carry_2 = jnp.where(y <= 1, 1.0, 0.0)

    def send_rows(msg, j):
        return rows((msg * NCH + j) * 256, 256)

    def push_copy(msg, j):
        return remote(
            pb.at[send_rows(msg, j), :], rb.at[send_rows(msg, j), :],
            push_send.at[msg, j], push_recv.at[msg, j], push_to[msg],
        )

    def weight_copy(msg):
        return remote(
            wsend.at[msg], wrecv.at[msg], wp_send.at[msg], wp_recv.at[msg], push_to[msg]
        )

    weight = jnp.full((8, 128), pw_ref[0], F32)
    share = weight * inv_den[:, :128]
    for msg in range(4):
        wsend[msg] = share * link[msg]
    for msg in range(3):
        weight_copy(msg).start()

    def push_first(j, carry):
        cols = rows(j * CH, CH)
        gradient = dot_nn(ot[...], cotb[:, cols])
        half_step = numb[:, cols].astype(F32) - STEP_SIZE * gradient
        acc[rows(j * 256, 256), :] = half_step * kept
        sending = half_step * inv_den
        for msg in range(4):
            pb[send_rows(msg, j), :] = (sending * link[msg]).astype(BF)
        for msg in range(3):
            push_copy(msg, j).start()
        return carry

    lax.fori_loop(0, NCH, push_first, 0)

    for msg in range(2):
        weight_copy(msg).wait_recv()
    wsend[3] = wsend[3] + wrecv[0] * carry_1 + wrecv[1] * carry_2
    weight_copy(3).start()

    def push_second(j, carry):
        for msg in range(2):
            push_copy(msg, j).wait_recv()
        one = rb[send_rows(0, j), :].astype(F32)
        two = rb[send_rows(1, j), :].astype(F32)
        four = pb[send_rows(3, j), :].astype(F32)
        pb[send_rows(3, j), :] = (four + one * carry_1 + two * carry_2).astype(BF)
        push_copy(3, j).start()
        part = rows(j * 256, 256)
        acc[part, :] = acc[part, :] + one * from_1 + two * from_2
        return carry

    lax.fori_loop(0, NCH, push_second, 0)

    for msg in range(2, 4):
        weight_copy(msg).wait_recv()
    w_out[...] = (
        weight * kept[:, :128] + wrecv[0] * from_1 + wrecv[1] * from_2 + wrecv[2] + wrecv[3]
    )

    def mix_copy(j):
        cols = rows(j * CH, CH)
        return pltpu.make_async_copy(mixb.at[:, cols], mix_out.at[:, cols], mix_sem.at[j])

    def push_third(j, carry):
        for msg in range(2, 4):
            push_copy(msg, j).wait_recv()
        eight = rb[send_rows(2, j), :].astype(F32)
        four = rb[send_rows(3, j), :].astype(F32)
        mixb[:, rows(j * CH, CH)] = (acc[rows(j * 256, 256), :] + eight + four).astype(BF)
        mix_copy(j).start()
        return carry

    lax.fori_loop(0, NCH, push_third, 0)

    def wait_mix(j, carry):
        mix_copy(j).wait()
        for msg in range(4):
            push_copy(msg, j).wait_send()
        return carry

    lax.fori_loop(0, NCH, wait_mix, 0)
    for msg in range(4):
        weight_copy(msg).wait_send()

    def wait_ring(s, carry):
        for sub in range(2):
            sib_copy(s, sub).wait_send()

            @pl.when(s < 7)
            def _():
                ring_copy(s, sub).wait_send()

        return carry

    lax.fori_loop(0, 8, wait_ring, 0)

    def wait_out(step, carry):
        dst = mod(me + step, 16)
        src = mod(me - step + 16, 16)
        for t in range(3):
            in_copy(t, dst, src).wait_send()
            out_copy(t, dst, src).wait_send()
            out_copy(t, dst, src).wait_recv()
        return carry

    lax.fori_loop(1, 16, wait_out, 0)
    for t in range(3):
        out_own(t).wait()


def body(
    queries, key_rows, value_rows, cotangent, numerators, push_weights, doc_ids, out_links,
    denominators,
):
    any_space = pl.BlockSpec(memory_space=pl.ANY)
    in_vmem = pl.BlockSpec(memory_space=pltpu.VMEM)
    in_smem = pl.BlockSpec(memory_space=pltpu.SMEM)
    dma = pltpu.SemaphoreType.DMA
    dq, dk, dv, mixed, weights = pl.pallas_call(
        kernel,
        out_shape=(
            jax.ShapeDtypeStruct((TOK, 16 * FW), BF),
            jax.ShapeDtypeStruct((TOK, 16 * FW), BF),
            jax.ShapeDtypeStruct((TOK, 16 * FW), BF),
            jax.ShapeDtypeStruct((FW, OUTW), BF),
            jax.ShapeDtypeStruct((8, 128), F32),
        ),
        in_specs=[any_space] * 5 + [in_vmem] + [in_smem] * 3,
        out_specs=(any_space,) * 4 + (in_vmem,),
        scratch_shapes=[
            pltpu.VMEM((SEQ, FW), BF),
            pltpu.VMEM((PAD + SEQ, FW), BF),
            pltpu.VMEM((PAD + SEQ, FW), BF),
            pltpu.VMEM((FW, PAD + SEQ), BF),
            pltpu.VMEM((FW, PAD + SEQ), BF),
            pltpu.VMEM((16 * WIN * 256, 256), BF),
            pltpu.VMEM((2, WIN * 256, 256), F32),
            pltpu.VMEM((FW, SEQ), BF),
            pltpu.VMEM((SEQ, OUTW), BF),
            pltpu.VMEM((FW, OUTW), BF),
            pltpu.VMEM((FW, OUTW), BF),
            pltpu.VMEM((2 * (PAD + SEQ), FW), F32),
            pltpu.VMEM((SEQ, FW), BF),
            pltpu.VMEM((SEQ, FW), BF),
            pltpu.VMEM((SEQ, FW), BF),
            pltpu.VMEM((PAD + SEQ, 128), F32),
            pltpu.VMEM((4 * NCH * 256, 256), BF),
            pltpu.VMEM((FW, OUTW), BF),
            pltpu.VMEM((4, 8, 128), F32),
            pltpu.VMEM((4, 8, 128), F32),
            dma((8,)),
            dma((3, 16)),
            dma((3, 16)),
            dma((8, 2)),
            dma((8, 2)),
            dma((8, 2)),
            dma((8, 2)),
            dma((3, 16)),
            dma((3, 16)),
            dma((4, NCH)),
            dma((4, NCH)),
            dma((4,)),
            dma((4,)),
            dma((NCH,)),
        ],
        compiler_params=pltpu.CompilerParams(
            collective_id=0, has_side_effects=True, vmem_limit_bytes=63 * 1024 * 1024
        ),
        name="push_step",
    )(
        queries[0], key_rows[0], value_rows[0], cotangent[0], numerators[0], doc_ids,
        push_weights, out_links, denominators,
    )
    return (dq[None], dk[None], dv[None], mixed[None], weights[0, :1])


def solution(mesh):
    tokens = P("rep", "seq", None)
    return jax.shard_map(
        body,
        mesh=mesh,
        in_specs=(tokens,) * 5 + (P("rep"), P("rep", None), P(), P()),
        out_specs=(tokens,) * 4 + (P("rep"),),
        check_vma=False,
    )
```

time: 584 us -> 283 us (0.48)
  the two profiles are of different devices: /device:TPU:12 before, /device:TPU:1 now
where the time goes in v1:
time: 283 us
  Pallas kernels  274 us (97%)
  local copies, waits for them, and re-layouts  6.84 us (2%)
    pallas_call x1, Pallas kernels, body(): pl.pallas_call(kernel, out_shape=(jax.ShapeDtypeStruct((TOK, 16 * FW), BF...  274 us

profile of v1, /device:TPU:1, one launch (start us, length us, event | category | flops | bytes accessed | tf_op | source)
XLA Modules:
  0.0 282.6 jit_solution(13859894577228240780)
XLA Ops:
  1.3 274.5 %push_step.1 = (bf16[128,4096]{1,0:T(8,128)(2,1)}, bf16[128,4096]{1,0:T(8,128)(2,1)}, bf16[128,4096]{1,0:T(8,128)(2,1)}, bf16[256,3584]{1,0:T(8,128)(2,1)}, f32[8,128]{1,0:T(8,128)}) custom-call(bf16[128,4096]{1,0:T(8,128)(2,1)} %bitcast.12, bf16[128,4096]{1,0:T(8,128)(2,1)} %bitcast.13, bf16[128,4096]{1,0:T(8,128)(2,1)} %bitcast.14, ...), custom_call_target="tpu_custom_call" | custom-call | tf_op jit(solution)/shard_map/push_step/pallas_call | solution.py:459
  275.8 0.0 copy-start.2
  275.8 1.3 slice.3
  277.1 0.0 copy-start.1
  277.1 2.4 copy.19
  279.4 0.0 copy-done.2
  279.5 0.0 copy-start
  279.5 1.0 copy.20
  280.4 0.0 copy-done.1
  280.4 1.0 copy.21
  281.4 0.0 copy-done
  281.4 1.2 copy.22
Async XLA Ops:
  275.8 3.7 %copy-start.2 = (bf16[128,4096]{1,0:T(8,128)(2,1)S(1)}, bf16[128,4096]{1,0:T(8,128)(2,1)}, u32[]{:S(2)}) copy-start(bf16[128,4096]{1,0:T(8,128)(2,1)} %get-tuple-element.11) | copy-start | bytes 3145732
  277.1 3.4 %copy-start.1 = (bf16[128,4096]{1,0:T(8,128)(2,1)S(1)}, bf16[128,4096]{1,0:T(8,128)(2,1)}, u32[]{:S(2)}) copy-start(bf16[128,4096]{1,0:T(8,128)(2,1)} %get-tuple-element.12) | copy-start | bytes 3145732
  279.5 1.9 copy-start

commit v2 on v1

v2 whole, which is shorter than its diff:
```python
import math

import jax
import jax.numpy as jnp
from jax import lax
from jax.experimental import pallas as pl
from jax.experimental.pallas import tpu as pltpu
from jax.sharding import PartitionSpec as P

HD = 128
SEQ = 2048
TOK = 128
OUTW = 3584
FW = 256
REACH = 4
WIN = REACH + 1
PAD = REACH * 256
CH = 256
NCH = OUTW // CH
HALF = OUTW // 2
STEP_SIZE = 3.0
SCALE = 1.0 / math.sqrt(HD)
EXP2_SCALE = SCALE * math.log2(math.e)
NEG = -1e30
MESH = pl.DeviceIdType.MESH
BF = jnp.bfloat16
F32 = jnp.float32


def mod(a, n):
    return lax.rem(a, n)


def dot_nn(a, b):
    return lax.dot_general(a, b, (((1,), (0,)), ((), ())), preferred_element_type=F32)


def dot_nt(a, b):
    return lax.dot_general(a, b, (((1,), (1,)), ((), ())), preferred_element_type=F32)


def rows(start, size):
    return pl.ds(pl.multiple_of(start, size), size)


def kernel(
    q_ref, k_ref, v_ref, cot_ref, num_ref, doc_ref, pw_ref, links_ref, den_ref,
    dq_out, dk_out, dv_out, mix_out, w_out,
    qh, kp, vp, kt, vt, pb, sbuf, ot, cotb, numb, debt, acc, base, dqb, dvb, dcol,
    outgo, rb, relay, wsend, wrecv,
    loc_sem, in_send, in_recv, ring_send, ring_recv, sib_send, sib_recv,
    out_send, out_recv, push_send, push_recv, relay_send, relay_recv, wp_send, wp_recv, mix_sem,
):
    rep = lax.axis_index("rep")
    me = lax.axis_index("seq")
    x, y = lax.div(rep, 4), mod(rep, 4)
    z, core = lax.div(me, 2), mod(me, 2)
    way = 1 - 2 * core
    sibling = (rep, z * 2 + 1 - core)
    ring_next = (rep, mod(z + way + 8, 8) * 2 + core)

    def at_xy(dx, dy):
        return (mod(x + dx + 4, 4) * 4 + mod(y + dy + 4, 4), me)

    push_to = (at_xy(0, 1), at_xy(0, 2), at_xy(2, 0), at_xy(1, 0))
    relay_to = (at_xy(0, -1), at_xy(-1, 0))

    barrier = pltpu.get_barrier_semaphore()
    for step in range(1, 16):
        pl.semaphore_signal(
            barrier, inc=1, device_id=(rep, mod(me + step, 16)), device_id_type=MESH
        )
    for dx, dy in ((0, 1), (0, 2), (0, 3), (1, 0), (2, 0), (3, 0)):
        pl.semaphore_signal(barrier, inc=1, device_id=at_xy(dx, dy), device_id_type=MESH)
    pl.semaphore_wait(barrier, 21)

    def remote(src, dst, send, recv, device):
        return pltpu.make_async_remote_copy(
            src_ref=src, dst_ref=dst, send_sem=send, recv_sem=recv, device_id=device,
            device_id_type=MESH,
        )

    heads_in = ((q_ref, qh, 0), (k_ref, kp, PAD), (v_ref, vp, PAD))

    def in_copy(t, dst, src):
        source, target, base = heads_in[t]
        return remote(
            source.at[:, rows(dst * FW, FW)],
            target.at[pl.ds(pl.multiple_of(base + src * TOK, TOK), TOK), :],
            in_send.at[t, dst], in_recv.at[t, src], (rep, dst),
        )

    def in_own(t):
        source, target, base = heads_in[t]
        return pltpu.make_async_copy(
            source.at[:, rows(me * FW, FW)],
            target.at[pl.ds(pl.multiple_of(base + me * TOK, TOK), TOK), :],
            loc_sem.at[t],
        )

    own_cot = pltpu.make_async_copy(cot_ref, cotb.at[rows(me * TOK, TOK), :], loc_sem.at[3])
    own_num = pltpu.make_async_copy(num_ref, numb, loc_sem.at[4])

    def send_in(step, carry):
        dst = mod(me + step, 16)
        for t in range(3):
            in_copy(t, dst, me).start()
        return carry

    own_num.start()
    own_cot.start()
    def ring_block(step):
        return mod(z - way * step + 8, 8) * 2 + core

    def sib_block(step):
        return mod(z + way * step + 8, 8) * 2 + 1 - core

    def piece(part, block, sub):
        return cotb.at[
            pl.ds(pl.multiple_of(block * TOK + sub * 64, 64), 64),
            part * HALF:(part + 1) * HALF,
        ]

    def ring_copy(part, step, sub):
        ref = piece(part, ring_block(step), sub)
        return remote(
            ref, ref, ring_send.at[part, step, sub], ring_recv.at[part, step + 1, sub], ring_next
        )

    def ring_arrival(part, step, sub):
        ref = piece(part, ring_block(step), sub)
        return remote(
            ref, ref, ring_send.at[part, step, sub], ring_recv.at[part, step, sub], ring_next
        )

    def sib_copy(part, step, sub):
        ref = piece(part, ring_block(step), sub)
        return remote(
            ref, ref, sib_send.at[part, step, sub], sib_recv.at[part, step, sub], sibling
        )

    def sib_arrival(part, step, sub):
        ref = piece(part, sib_block(step), sub)
        return remote(
            ref, ref, sib_send.at[part, step, sub], sib_recv.at[part, step, sub], sibling
        )

    def first_sends(part):
        for sub in range(2):
            ring_copy(part, 0, sub).start()
            sib_copy(part, 0, sub).start()

    def take(part, step):
        for sub in range(2):
            ring_arrival(part, step, sub).wait_recv()

            @pl.when(step < 7)
            def _():
                ring_copy(part, step, sub).start()

            sib_copy(part, step, sub).start()

    lax.fori_loop(1, 16, send_in, 0)
    for t in range(3):
        in_own(t).start()
    own_cot.wait()
    first_sends(0)

    kp[0:PAD, :] = jnp.zeros((PAD, FW), BF)
    vp[0:PAD, :] = jnp.zeros((PAD, FW), BF)
    dcol[0:PAD, :] = jnp.full((PAD, 128), -1.0, F32)

    def zero_acc(i, carry):
        acc[rows(i * 256, 256), :] = jnp.zeros((256, FW), F32)
        return carry

    lax.fori_loop(0, acc.shape[0] // 256, zero_acc, 0)

    def doc_columns(i, carry):
        part = doc_ref[:, rows(i * 128, 128)].astype(F32)
        dcol[pl.ds(pl.multiple_of(PAD + i * 128, 128), 128), :] = jnp.broadcast_to(
            part, (128, 128)
        ).T
        return carry

    lax.fori_loop(0, SEQ // 128, doc_columns, 0)
    own_num.wait()
    inv_weight = 1.0 / jnp.full((1, CH), pw_ref[0], F32)

    def debias(j, carry):
        cols = rows(j * CH, CH)
        debt[cols, :] = (numb[:, cols].astype(F32) * inv_weight).T.astype(BF)
        return carry

    lax.fori_loop(0, NCH, debias, 0)

    link = [links_ref[rep, mod(rep + off, 16)].astype(F32) for off in (1, 2, 8, 4)]
    inv_den = 1.0 / jnp.full((1, CH), den_ref[rep].astype(F32), F32)
    links_out = links_ref[rep, 0]
    for col in range(1, 16):
        links_out = links_out + links_ref[rep, col]
    kept = 1.0 - jnp.full((1, CH), links_out.astype(F32), F32) * inv_den
    def taken(dx, dy, off):
        source = at_xy(dx, dy)[0]
        return links_ref[source, mod(source + off, 16)].astype(F32)

    taken_1, taken_2, taken_8 = taken(0, -1, 1), taken(0, -2, 2), taken(-2, 0, 8)
    from_1 = jnp.where(y >= 1, 1.0, 0.0)
    from_2 = jnp.where(y >= 2, 1.0, 0.0)
    carry_1 = jnp.where(y == 0, 1.0, 0.0)
    carry_2 = jnp.where(y <= 1, 1.0, 0.0)

    def weight_copy(msg):
        return remote(
            wsend.at[msg], wrecv.at[msg], wp_send.at[msg], wp_recv.at[msg], push_to[msg]
        )

    weight = jnp.full((8, 128), pw_ref[0], F32)
    share = weight * inv_den[:, :128]
    for msg in range(4):
        wsend[msg] = share * link[msg]
    for msg in range(3):
        weight_copy(msg).start()

    for msg in range(2):
        weight_copy(msg).wait_recv()
    wsend[3] = wsend[3] + wrecv[0] * carry_1 + wrecv[1] * carry_2
    weight_copy(3).start()

    take(0, jnp.int32(1))

    def wait_in(step, carry):
        src = mod(me - step + 16, 16)
        for t in range(3):
            in_copy(t, mod(me + step, 16), src).wait_recv()
        return carry

    for t in range(3):
        in_own(t).wait()
    lax.fori_loop(1, 16, wait_in, 0)

    def flip(i, carry):
        cols = rows(i * 256, 256)
        kt[:, cols] = kp[cols, :].T
        vt[:, cols] = vp[cols, :].T
        return carry

    lax.fori_loop(0, (PAD + SEQ) // 256, flip, 0)

    later_key = lax.broadcasted_iota(jnp.int32, (256, 256), 0) <= lax.broadcasted_iota(
        jnp.int32, (256, 256), 1
    )

    def prob_rows(a, h, c):
        slot = mod(a - z + 14, 8)
        return rows(((slot * 2 + h) * WIN + c) * 256, 256)

    def forward(a):
        doc_q = doc_ref[:, rows(a * 256, 256)].astype(F32)
        for h in range(2):
            feats = slice(h * HD, (h + 1) * HD)
            qa = qh[rows(a * 256, 256), feats]
            peak = jnp.full((1, 256), NEG, F32)
            for c in range(WIN):
                keys = rows((a + c) * 256, 256)
                scores = dot_nt(kp[keys, feats], qa)
                dk_col = dcol[keys, :]
                allowed = jnp.concatenate([dk_col, dk_col], axis=1) == doc_q
                if c == REACH:
                    allowed = allowed & later_key
                scores = jnp.where(allowed, scores, NEG)
                sbuf[c * 256:(c + 1) * 256, :] = scores
                peak = jnp.maximum(peak, jnp.max(scores, axis=0, keepdims=True))
            total = jnp.zeros((1, 256), F32)
            for c in range(WIN):
                part = slice(c * 256, (c + 1) * 256)
                expo = jnp.exp2((sbuf[part, :] - peak) * EXP2_SCALE)
                sbuf[part, :] = expo
                total = total + jnp.sum(expo, axis=0, keepdims=True)
            inv_total = 1.0 / total
            out = jnp.zeros((HD, 256), F32)
            for c in range(WIN):
                probs = (sbuf[c * 256:(c + 1) * 256, :] * inv_total).astype(BF)
                pb[prob_rows(a, h, c), :] = probs
                out = out + dot_nn(vt[feats, rows((a + c) * 256, 256)], probs)
            ot[feats, rows(a * 256, 256)] = out.astype(BF)

    def out_copy(t, dst, src):
        source, target = ((dqb, dq_out), (qh, dk_out), (dvb, dv_out))[t]
        return remote(
            source.at[rows(dst * TOK, TOK), :], target.at[:, rows(src * FW, FW)],
            out_send.at[t, dst], out_recv.at[t, src], (rep, dst),
        )

    def out_own(t):
        source, target = ((dqb, dq_out), (qh, dk_out), (dvb, dv_out))[t]
        return pltpu.make_async_copy(
            source.at[rows(me * TOK, TOK), :], target.at[:, rows(me * FW, FW)], loc_sem.at[5 + t]
        )

    def backward(a, half, grad):
        tok = rows((a * 2 + half) * TOK, TOK)
        lanes = slice(half * TOK, (half + 1) * TOK)
        for h in range(2):
            feats = slice(h * HD, (h + 1) * HD)
            go = grad[lanes, feats]
            go_rows = go.T.astype(BF)
            go = go.astype(BF)
            centre = jnp.sum(
                go_rows.astype(F32) * ot[feats, tok].astype(F32), axis=0, keepdims=True
            )
            qa = qh[tok, feats]
            dq = jnp.zeros((HD, TOK), F32)
            for c in range(WIN):
                keys = rows((a + c) * 256, 256)
                probs = pb[prob_rows(a, h, c), lanes]
                grad_probs = dot_nn(vp[keys, feats], go_rows)
                grad_scores = (probs.astype(F32) * (grad_probs - centre)).astype(BF)
                v_rows = pl.ds(pl.multiple_of(PAD + SEQ + (a + c) * 256, 256), 256)
                acc[keys, feats] += dot_nn(grad_scores, qa)
                acc[v_rows, feats] += dot_nn(probs, go)
                dq = dq + dot_nn(kt[feats, keys], grad_scores)
            dqb[tok, feats] = (dq * SCALE).T.astype(BF)

    def block_of(step, half):
        return mod(z + (2 * half - 1) * step + 8, 8) * 2 + half

    def send_dq(step, half):
        device = block_of(step, half)

        @pl.when(device != me)
        def _():
            out_copy(0, device, me).start()

        @pl.when(device == me)
        def _():
            out_own(0).start()

    def compute(s):
        blocks = [block_of(s, half) for half in range(2)]
        both = jnp.concatenate([cotb[rows(b * TOK, TOK), :] for b in blocks], axis=0)
        grad = dot_nn(both, debt[...])
        for half in range(2):
            backward(lax.div(blocks[half], 2), half, grad)

    def forward_step(b, carry):
        forward(b)

        @pl.when(b <= 5)
        def _():
            take(0, b + 2)

        @pl.when(b == 4)
        def _():
            first_sends(1)

        return carry

    def wait_sib(part, step):
        for sub in range(2):
            sib_arrival(part, step, sub).wait_recv()

    def wait_sib_all(step, carry):
        wait_sib(0, step)
        return carry

    def ring_step(s, carry):
        @pl.when(s < 7)
        def _():
            take(1, s + 1)
            wait_sib(1, s)

        @pl.when(s == 3)
        def _():
            lax.fori_loop(0, NCH // 4, relay_step, 0)

        @pl.when(s == 6)
        def _():
            wait_sib(1, 7)
            lax.fori_loop(NCH // 2, NCH, push_first, 0)

        @pl.when(s == 7)
        def _():
            lax.fori_loop(0, NCH // 2, push_second, 0)

        compute(s)
        for half in range(2):
            send_dq(s, half)
        return carry

    def slot_rows(msg, j):
        return rows((msg * NCH + j) * 256, 256)

    def outgoing(msg, j):
        part = rows(j * 256, 256)
        return pb.at[part, :] if msg == 3 else outgo.at[part, :]

    def direct(msg, j):
        return remote(
            outgoing(msg, j), rb.at[slot_rows(msg, j), :],
            push_send.at[msg, j], push_recv.at[msg, j], push_to[msg],
        )

    def arrival(msg, j):
        return direct(msg, j)

    def relay_rows(way_round, i):
        return rows((way_round * (NCH // 2) + i) * 256, 256)

    def relay_in(way_round, i):
        return remote(
            outgoing(way_round + 1, 2 * i + 1), relay.at[relay_rows(way_round, i), :],
            push_send.at[way_round + 1, 2 * i + 1], relay_recv.at[way_round, i], relay_to[way_round],
        )

    def relay_on(way_round, i):
        return remote(
            relay.at[relay_rows(way_round, i), :], rb.at[slot_rows(way_round + 1, 2 * i + 1), :],
            relay_send.at[way_round, i], push_recv.at[way_round + 1, 2 * i + 1],
            relay_to[way_round],
        )

    def push_first(j, carry):
        cols = rows(j * CH, CH)
        gradient = dot_nn(ot[...], cotb[:, cols])
        half_step = numb[:, cols].astype(F32) - STEP_SIZE * gradient
        base[rows(j * 256, 256), :] = half_step * kept
        outgo[rows(j * 256, 256), :] = (half_step * inv_den).astype(BF)
        direct(0, j).start()

        @pl.when(mod(j, 2) == 0)
        def _():
            for way_round in range(2):
                direct(way_round + 1, j).start()

        @pl.when(mod(j, 2) == 1)
        def _():
            for way_round in range(2):
                relay_in(way_round, lax.div(j, 2)).start()

        return carry

    def relay_step(i, carry):
        for way_round in range(2):
            relay_in(way_round, i).wait_recv()
            relay_on(way_round, i).start()
        return carry

    def push_second(j, carry):
        for msg in range(2):
            arrival(msg, j).wait_recv()
        one = rb[slot_rows(0, j), :].astype(F32)
        two = rb[slot_rows(1, j), :].astype(F32)
        part = rows(j * 256, 256)
        four = outgo[part, :].astype(F32) * link[3]
        pb[part, :] = (four + one * (taken_1 * carry_1) + two * (taken_2 * carry_2)).astype(BF)
        direct(3, j).start()
        base[part, :] = base[part, :] + one * (taken_1 * from_1) + two * (taken_2 * from_2)
        return carry

    lax.fori_loop(0, 8, forward_step, 0)
    lax.fori_loop(0, 8, wait_sib_all, 0)
    lax.fori_loop(0, NCH // 2, push_first, 0)
    lax.fori_loop(0, 8, ring_step, 0)

    def finish(i, carry):
        dst = mod(me + i, 16)
        tok = rows(dst * TOK, TOK)
        qh[tok, :] = (
            acc[pl.ds(pl.multiple_of(PAD + dst * TOK, TOK), TOK), :] * SCALE
        ).astype(BF)
        dvb[tok, :] = acc[
            pl.ds(pl.multiple_of(2 * PAD + SEQ + dst * TOK, TOK), TOK), :
        ].astype(BF)

        @pl.when(i > 0)
        def _():
            out_copy(1, dst, me).start()
            out_copy(2, dst, me).start()

        @pl.when(i == 0)
        def _():
            out_own(1).start()
            out_own(2).start()

        return carry

    lax.fori_loop(0, 16, finish, 0)

    lax.fori_loop(NCH // 4, NCH // 2, relay_step, 0)
    lax.fori_loop(NCH // 2, NCH, push_second, 0)

    for msg in range(2, 4):
        weight_copy(msg).wait_recv()
    w_out[...] = (
        weight * kept[:, :128] + wrecv[0] * from_1 + wrecv[1] * from_2 + wrecv[2] + wrecv[3]
    )

    def mix_copy(j):
        cols = rows(j * CH, CH)
        return pltpu.make_async_copy(numb.at[:, cols], mix_out.at[:, cols], mix_sem.at[j])

    def push_third(j, carry):
        for msg in range(2, 4):
            arrival(msg, j).wait_recv()
        eight = rb[slot_rows(2, j), :].astype(F32)
        four = rb[slot_rows(3, j), :].astype(F32)
        numb[:, rows(j * CH, CH)] = (
            base[rows(j * 256, 256), :] + eight * taken_8 + four
        ).astype(BF)
        mix_copy(j).start()
        return carry

    lax.fori_loop(0, NCH, push_third, 0)

    def wait_mix(j, carry):
        mix_copy(j).wait()
        for msg in range(4):
            direct(msg, j).wait_send()
        return carry

    lax.fori_loop(0, NCH, wait_mix, 0)

    def wait_relay(i, carry):
        for way_round in range(2):
            relay_on(way_round, i).wait_send()
        return carry

    lax.fori_loop(0, NCH // 2, wait_relay, 0)
    for msg in range(4):
        weight_copy(msg).wait_send()

    def wait_ring(s, carry):
        for part in range(2):
            for sub in range(2):
                sib_copy(part, s, sub).wait_send()

                @pl.when(s < 7)
                def _():
                    ring_copy(part, s, sub).wait_send()

        return carry

    lax.fori_loop(0, 8, wait_ring, 0)

    def wait_out(step, carry):
        dst = mod(me + step, 16)
        src = mod(me - step + 16, 16)
        for t in range(3):
            in_copy(t, dst, src).wait_send()
            out_copy(t, dst, src).wait_send()
            out_copy(t, dst, src).wait_recv()
        return carry

    lax.fori_loop(1, 16, wait_out, 0)
    for t in range(3):
        out_own(t).wait()


def body(
    queries, key_rows, value_rows, cotangent, numerators, push_weights, doc_ids, out_links,
    denominators,
):
    any_space = pl.BlockSpec(memory_space=pl.ANY)
    in_vmem = pl.BlockSpec(memory_space=pltpu.VMEM)
    in_smem = pl.BlockSpec(memory_space=pltpu.SMEM)
    dma = pltpu.SemaphoreType.DMA
    dq, dk, dv, mixed, weights = pl.pallas_call(
        kernel,
        out_shape=(
            jax.ShapeDtypeStruct((TOK, 16 * FW), BF),
            jax.ShapeDtypeStruct((TOK, 16 * FW), BF),
            jax.ShapeDtypeStruct((TOK, 16 * FW), BF),
            jax.ShapeDtypeStruct((FW, OUTW), BF),
            jax.ShapeDtypeStruct((8, 128), F32),
        ),
        in_specs=[any_space] * 5 + [in_vmem] + [in_smem] * 3,
        out_specs=(any_space,) * 4 + (in_vmem,),
        scratch_shapes=[
            pltpu.VMEM((SEQ, FW), BF),
            pltpu.VMEM((PAD + SEQ, FW), BF),
            pltpu.VMEM((PAD + SEQ, FW), BF),
            pltpu.VMEM((FW, PAD + SEQ), BF),
            pltpu.VMEM((FW, PAD + SEQ), BF),
            pltpu.VMEM((16 * WIN * 256, 256), BF),
            pltpu.VMEM((WIN * 256, 256), F32),
            pltpu.VMEM((FW, SEQ), BF),
            pltpu.VMEM((SEQ, OUTW), BF),
            pltpu.VMEM((FW, OUTW), BF),
            pltpu.VMEM((OUTW, FW), BF),
            pltpu.VMEM((2 * (PAD + SEQ), FW), F32),
            pltpu.VMEM((NCH * 256, 256), F32),
            pltpu.VMEM((SEQ, FW), BF),
            pltpu.VMEM((SEQ, FW), BF),
            pltpu.VMEM((PAD + SEQ, 128), F32),
            pltpu.VMEM((NCH * 256, 256), BF),
            pltpu.VMEM((4 * NCH * 256, 256), BF),
            pltpu.VMEM((NCH * 256, 256), BF),
            pltpu.VMEM((4, 8, 128), F32),
            pltpu.VMEM((4, 8, 128), F32),
            dma((8,)),
            dma((3, 16)),
            dma((3, 16)),
            dma((2, 8, 2)),
            dma((2, 8, 2)),
            dma((2, 8, 2)),
            dma((2, 8, 2)),
            dma((3, 16)),
            dma((3, 16)),
            dma((4, NCH)),
            dma((4, NCH)),
            dma((2, NCH // 2)),
            dma((2, NCH // 2)),
            dma((4,)),
            dma((4,)),
            dma((NCH,)),
        ],
        compiler_params=pltpu.CompilerParams(
            collective_id=0, has_side_effects=True, vmem_limit_bytes=63 * 1024 * 1024
        ),
        name="push_step",
    )(
        queries[0], key_rows[0], value_rows[0], cotangent[0], numerators[0], doc_ids,
        push_weights, out_links, denominators,
    )
    return (dq[None], dk[None], dv[None], mixed[None], weights[0, :1])


def solution(mesh):
    tokens = P("rep", "seq", None)
    return jax.shard_map(
        body,
        mesh=mesh,
        in_specs=(tokens,) * 5 + (P("rep"), P("rep", None), P(), P()),
        out_specs=(tokens,) * 4 + (P("rep"),),
        check_vma=False,
    )
```

time: 283 us -> 251 us (0.89)
  Pallas kernels: 274 us -> 242 us
    pallas_call x1, Pallas kernels: 274 us -> 242 us  [body(): pl.pallas_call(kernel, out_shape=(jax.ShapeDtypeStruct((TOK, 16 * FW), BF...]
where the time goes in v2:
time: 251 us; the launch traced here: 250 us
  Pallas kernels  242 us (96%)
  local copies, waits for them, and re-layouts  6.84 us (3%)
    pallas_call x1, Pallas kernels, body(): pl.pallas_call(kernel, out_shape=(jax.ShapeDtypeStruct((TOK, 16 * FW), BF...  242 us
    unnamed x10, local copies, waits for them, and re-layouts  5.56 us

profile of v2, /device:TPU:1, one launch (start us, length us, event | category | flops | bytes accessed | tf_op | source)
XLA Modules:
  0.0 250.3 jit_solution(14356107485002474047)
XLA Ops:
  1.3 242.2 %push_step.1 = (bf16[128,4096]{1,0:T(8,128)(2,1)}, bf16[128,4096]{1,0:T(8,128)(2,1)}, bf16[128,4096]{1,0:T(8,128)(2,1)}, bf16[256,3584]{1,0:T(8,128)(2,1)}, f32[8,128]{1,0:T(8,128)}) custom-call(bf16[128,4096]{1,0:T(8,128)(2,1)} %bitcast.12, bf16[128,4096]{1,0:T(8,128)(2,1)} %bitcast.13, bf16[128,4096]{1,0:T(8,128)(2,1)} %bitcast.14, ...), custom_call_target="tpu_custom_call" | custom-call | tf_op jit(solution)/shard_map/push_step/pallas_call | solution.py:568
  243.4 0.0 copy-start.2
  243.4 1.3 slice.3
  244.7 0.0 copy-start.1
  244.7 2.4 copy.19
  247.1 0.0 copy-done.2
  247.1 0.0 copy-start
  247.1 1.0 copy.20
  248.1 0.0 copy-done.1
  248.1 1.0 copy.21
  249.1 0.0 copy-done
  249.1 1.2 copy.22
Async XLA Ops:
  243.4 3.7 %copy-start.2 = (bf16[128,4096]{1,0:T(8,128)(2,1)S(1)}, bf16[128,4096]{1,0:T(8,128)(2,1)}, u32[]{:S(2)}) copy-start(bf16[128,4096]{1,0:T(8,128)(2,1)} %get-tuple-element.11) | copy-start | bytes 3145732
  244.7 3.4 %copy-start.1 = (bf16[128,4096]{1,0:T(8,128)(2,1)S(1)}, bf16[128,4096]{1,0:T(8,128)(2,1)}, u32[]{:S(2)}) copy-start(bf16[128,4096]{1,0:T(8,128)(2,1)} %get-tuple-element.12) | copy-start | bytes 3145732
  247.1 1.9 copy-start

commit v3 on v2

--- a/solution.py
+++ b/solution.py
@@ -17,7 +17,9 @@
 PAD = REACH * 256
 CH = 256
 NCH = OUTW // CH
-HALF = OUTW // 2
+FIRST = 5
+HALF = FIRST * CH
+COLS = (slice(0, HALF), slice(HALF, OUTW))
 STEP_SIZE = 3.0
 SCALE = 1.0 / math.sqrt(HD)
 EXP2_SCALE = SCALE * math.log2(math.e)
@@ -46,7 +48,7 @@
 def kernel(
     q_ref, k_ref, v_ref, cot_ref, num_ref, doc_ref, pw_ref, links_ref, den_ref,
     dq_out, dk_out, dv_out, mix_out, w_out,
-    qh, kp, vp, kt, vt, pb, sbuf, ot, cotb, numb, debt, acc, base, dqb, dvb, dcol,
+    qh, kp, vp, kt, vt, pb, sbuf, ot, cotb, numb, debt, acc, base, dqb, part_grad, dcol,
     outgo, rb, relay, wsend, wrecv,
     loc_sem, in_send, in_recv, ring_send, ring_recv, sib_send, sib_recv,
     out_send, out_recv, push_send, push_recv, relay_send, relay_recv, wp_send, wp_recv, mix_sem,
@@ -118,7 +120,7 @@
     def piece(part, block, sub):
         return cotb.at[
             pl.ds(pl.multiple_of(block * TOK + sub * 64, 64), 64),
-            part * HALF:(part + 1) * HALF,
+            COLS[part],
         ]
 
     def ring_copy(part, step, sub):
@@ -286,14 +288,14 @@
             ot[feats, rows(a * 256, 256)] = out.astype(BF)
 
     def out_copy(t, dst, src):
-        source, target = ((dqb, dq_out), (qh, dk_out), (dvb, dv_out))[t]
+        source, target = ((dqb, dq_out), (qh, dk_out), (kp, dv_out))[t]
         return remote(
             source.at[rows(dst * TOK, TOK), :], target.at[:, rows(src * FW, FW)],
             out_send.at[t, dst], out_recv.at[t, src], (rep, dst),
         )
 
     def out_own(t):
-        source, target = ((dqb, dq_out), (qh, dk_out), (dvb, dv_out))[t]
+        source, target = ((dqb, dq_out), (qh, dk_out), (kp, dv_out))[t]
         return pltpu.make_async_copy(
             source.at[rows(me * TOK, TOK), :], target.at[:, rows(me * FW, FW)], loc_sem.at[5 + t]
         )
@@ -336,12 +338,19 @@
         def _():
             out_own(0).start()
 
+    def both_blocks(step, part):
+        return jnp.concatenate(
+            [
+                cotb[rows(block_of(step, half) * TOK, TOK), COLS[part]]
+                for half in range(2)
+            ],
+            axis=0,
+        )
+
     def compute(s):
-        blocks = [block_of(s, half) for half in range(2)]
-        both = jnp.concatenate([cotb[rows(b * TOK, TOK), :] for b in blocks], axis=0)
-        grad = dot_nn(both, debt[...])
+        grad = part_grad[rows(s * 256, 256), :] + dot_nn(both_blocks(s, 1), debt[HALF:OUTW, :])
         for half in range(2):
-            backward(lax.div(blocks[half], 2), half, grad)
+            backward(lax.div(block_of(s, half), 2), half, grad)
 
     def forward_step(b, carry):
         forward(b)
@@ -354,34 +363,32 @@
         def _():
             first_sends(1)
 
+        wait_sib(0, b)
+        part_grad[rows(b * 256, 256), :] = dot_nn(both_blocks(b, 0), debt[0:HALF, :])
         return carry
 
     def wait_sib(part, step):
         for sub in range(2):
             sib_arrival(part, step, sub).wait_recv()
 
-    def wait_sib_all(step, carry):
-        wait_sib(0, step)
-        return carry
-
     def ring_step(s, carry):
         @pl.when(s < 7)
         def _():
             take(1, s + 1)
             wait_sib(1, s)
 
-        @pl.when(s == 3)
-        def _():
-            lax.fori_loop(0, NCH // 4, relay_step, 0)
+        @pl.when(s == 2)
+        def _():
+            lax.fori_loop(0, FIRST // 2, relay_step, 0)
+
+        @pl.when(s == 5)
+        def _():
+            lax.fori_loop(0, FIRST, push_second, 0)
 
         @pl.when(s == 6)
         def _():
             wait_sib(1, 7)
-            lax.fori_loop(NCH // 2, NCH, push_first, 0)
-
-        @pl.when(s == 7)
-        def _():
-            lax.fori_loop(0, NCH // 2, push_second, 0)
+            lax.fori_loop(FIRST, NCH, push_first, 0)
 
         compute(s)
         for half in range(2):
@@ -391,9 +398,13 @@
     def slot_rows(msg, j):
         return rows((msg * NCH + j) * 256, 256)
 
+    def joined_rows(j):
+        return rows((j + jnp.where(j < FIRST, 2 * 2 * WIN, -FIRST)) * 256, 256)
+
     def outgoing(msg, j):
-        part = rows(j * 256, 256)
-        return pb.at[part, :] if msg == 3 else outgo.at[part, :]
+        if msg == 3:
+            return pb.at[joined_rows(j), :]
+        return outgo.at[rows(j * 256, 256), :]
 
     def direct(msg, j):
         return remote(
@@ -453,14 +464,13 @@
         two = rb[slot_rows(1, j), :].astype(F32)
         part = rows(j * 256, 256)
         four = outgo[part, :].astype(F32) * link[3]
-        pb[part, :] = (four + one * (taken_1 * carry_1) + two * (taken_2 * carry_2)).astype(BF)
+        pb[joined_rows(j), :] = (four + one * (taken_1 * carry_1) + two * (taken_2 * carry_2)).astype(BF)
         direct(3, j).start()
         base[part, :] = base[part, :] + one * (taken_1 * from_1) + two * (taken_2 * from_2)
         return carry
 
     lax.fori_loop(0, 8, forward_step, 0)
-    lax.fori_loop(0, 8, wait_sib_all, 0)
-    lax.fori_loop(0, NCH // 2, push_first, 0)
+    lax.fori_loop(0, FIRST, push_first, 0)
     lax.fori_loop(0, 8, ring_step, 0)
 
     def finish(i, carry):
@@ -469,7 +479,7 @@
         qh[tok, :] = (
             acc[pl.ds(pl.multiple_of(PAD + dst * TOK, TOK), TOK), :] * SCALE
         ).astype(BF)
-        dvb[tok, :] = acc[
+        kp[tok, :] = acc[
             pl.ds(pl.multiple_of(2 * PAD + SEQ + dst * TOK, TOK), TOK), :
         ].astype(BF)
 
@@ -487,8 +497,8 @@
 
     lax.fori_loop(0, 16, finish, 0)
 
-    lax.fori_loop(NCH // 4, NCH // 2, relay_step, 0)
-    lax.fori_loop(NCH // 2, NCH, push_second, 0)
+    lax.fori_loop(FIRST // 2, NCH // 2, relay_step, 0)
+    lax.fori_loop(FIRST, NCH, push_second, 0)
 
     for msg in range(2, 4):
         weight_copy(msg).wait_recv()
@@ -591,7 +601,7 @@
             pltpu.VMEM((2 * (PAD + SEQ), FW), F32),
             pltpu.VMEM((NCH * 256, 256), F32),
             pltpu.VMEM((SEQ, FW), BF),
-            pltpu.VMEM((SEQ, FW), BF),
+            pltpu.VMEM((SEQ, FW), F32),
             pltpu.VMEM((PAD + SEQ, 128), F32),
             pltpu.VMEM((NCH * 256, 256), BF),
             pltpu.VMEM((4 * NCH * 256, 256), BF),

time: 251 us -> 250 us (level)
  no operation moved by 1% of the time
where the time goes in v3:
time: 250 us; the launch traced here: 249 us
  Pallas kernels  241 us (96%)
  local copies, waits for them, and re-layouts  6.84 us (3%)
    pallas_call x1, Pallas kernels, body(): pl.pallas_call(kernel, out_shape=(jax.ShapeDtypeStruct((TOK, 16 * FW), BF...  241 us
    unnamed x10, local copies, waits for them, and re-layouts  5.56 us

profile of v3, /device:TPU:1, one launch (start us, length us, event | category | flops | bytes accessed | tf_op | source)
XLA Modules:
  0.0 249.3 jit_solution(5672490244984487513)
XLA Ops:
  1.3 241.2 %push_step.1 = (bf16[128,4096]{1,0:T(8,128)(2,1)}, bf16[128,4096]{1,0:T(8,128)(2,1)}, bf16[128,4096]{1,0:T(8,128)(2,1)}, bf16[256,3584]{1,0:T(8,128)(2,1)}, f32[8,128]{1,0:T(8,128)}) custom-call(bf16[128,4096]{1,0:T(8,128)(2,1)} %bitcast.12, bf16[128,4096]{1,0:T(8,128)(2,1)} %bitcast.13, bf16[128,4096]{1,0:T(8,128)(2,1)} %bitcast.14, ...), custom_call_target="tpu_custom_call" | custom-call | tf_op jit(solution)/shard_map/push_step/pallas_call | solution.py:578
  242.5 0.0 copy-start.2
  242.5 1.3 slice.3
  243.7 0.0 copy-start.1
  243.7 2.4 copy.19
  246.1 0.0 copy-done.2
  246.1 0.0 copy-start
  246.1 1.0 copy.20
  247.1 0.0 copy-done.1
  247.1 1.0 copy.21
  248.1 0.0 copy-done
  248.1 1.2 copy.22
Async XLA Ops:
  242.5 3.7 %copy-start.2 = (bf16[128,4096]{1,0:T(8,128)(2,1)S(1)}, bf16[128,4096]{1,0:T(8,128)(2,1)}, u32[]{:S(2)}) copy-start(bf16[128,4096]{1,0:T(8,128)(2,1)} %get-tuple-element.11) | copy-start | bytes 3145732
  243.7 3.4 %copy-start.1 = (bf16[128,4096]{1,0:T(8,128)(2,1)S(1)}, bf16[128,4096]{1,0:T(8,128)(2,1)}, u32[]{:S(2)}) copy-start(bf16[128,4096]{1,0:T(8,128)(2,1)} %get-tuple-element.12) | copy-start | bytes 3145732
  246.1 1.9 copy-start
